TPU v7x, 256 devices: a whole 4x4x8 slice. The times are simulated.
256 devices in a mesh: seg: 16 (over z, core), bond: 16 (over x, y).
Axes of the slice: x: 4, y: 4, z: 8, core: 2. Of those that a mesh axis runs over, the one named last changes fastest.
Arguments:
- left_env: bfloat16 [16, 1024, 6, 1024], P('seg', 'bond'), may hold values from -0.1875 to 0.1875
- prev_left: bfloat16 [16, 1024, 1024], P('seg'), may hold values from -0.25 to 1.25
- cur_site: bfloat16 [16, 1024, 4, 1024], P('seg', 'bond'), may hold values from -6 to 6
- prev_site: bfloat16 [16, 1024, 4, 1024], P('seg', None, None, 'bond'), may hold values from -6 to 6
- hamiltonian: bfloat16 [16, 6, 6, 4, 4], P('seg'), may hold values from -1.25 to 1.25
- right_env: bfloat16 [16, 1024, 6, 1024], P('seg', 'bond'), may hold values from -0.078125 to 0.078125
- prev_right: bfloat16 [16, 1024, 1024], P('seg'), may hold values from -0.25 to 1.25
Outputs:
- new_site: bfloat16 [16, 1024, 4, 1024], P('seg', 'bond')
- center: float32 [16, 1024, 1024], P('seg', 'bond')
All inputs are finite; a program needn't handle non-finite values.
Results may differ from a plain program's by a relative error of at most 0.0054.
Values may be sent and summed in bfloat16 or wider, within the bound.
No kernel may reach another device: no remote copies, remote signals or barrier semaphores. Data moves between devices by JAX's collectives and lax.ppermute only.
A program may use at most 128 MiB of HBM per device.

v0:
```python
import math
import jax
import jax.numpy as jnp
from jax import lax
from jax.sharding import PartitionSpec as P

PHYS = 4
MPOB = 6


def shifted(block, axis, distance):
    devices = range(lax.axis_size(axis))
    route = [((i - distance) % len(devices), i) for i in devices]
    return lax.ppermute(block, axis, route)


def shards(left_env, prev_left, cur_site, prev_site, hamiltonian, right_env, prev_right):
    left_now, prev_now = shifted((left_env[0], prev_left[0]), "seg", 1)
    own_rows = left_now.shape[0]
    bond_width = left_now.shape[2]
    coupling = hamiltonian[0].astype(jnp.float32)
    current = lax.all_gather(cur_site[0], "bond", axis=0, tiled=True)
    projected = jnp.dot(
        left_now.reshape(own_rows * MPOB, bond_width),
        current.reshape(bond_width, PHYS * bond_width),
        preferred_element_type=jnp.float32,
    ).reshape(own_rows, MPOB, PHYS, bond_width)
    mixture = jnp.einsum(
        "autc,uvst->asvc", projected, coupling, precision=lax.Precision.HIGHEST
    ).astype(jnp.bfloat16)
    applied = jnp.einsum(
        "asvc,cvy->asy",
        mixture,
        lax.all_gather(right_env[0], "bond", axis=0, tiled=True),
        preferred_element_type=jnp.float32,
    )
    previous = lax.all_gather(prev_site[0], "bond", axis=2, tiled=True)
    own_left = lax.dynamic_slice_in_dim(prev_now, lax.axis_index("bond") * own_rows, own_rows, 0)
    partial_value = jnp.einsum(
        "ab,bsc->asc", own_left, previous, preferred_element_type=jnp.float32
    ).astype(jnp.bfloat16)
    second = jnp.einsum(
        "asc,cy->asy", partial_value, prev_right[0], preferred_element_type=jnp.float32
    )
    target = (2.0 * applied - second).reshape(own_rows * PHYS, bond_width)
    local_correlation = jnp.dot(
        target.T, target, precision=lax.Precision.HIGHEST, preferred_element_type=jnp.float32
    )
    correlation = lax.psum(local_correlation, "bond")
    triangle = jnp.linalg.cholesky(correlation)
    solved = jax.scipy.linalg.solve_triangular(triangle, target.T, lower=True)
    norming = math.sqrt(bond_width * PHYS)
    new_site = (solved.T * norming).astype(jnp.bfloat16).reshape(1, own_rows, PHYS, bond_width)
    offset = lax.axis_index("bond") * own_rows
    center = lax.dynamic_slice_in_dim(triangle.T, offset, own_rows, 0) / norming
    return (new_site, center[None])


def solution(mesh):
    return jax.shard_map(
        shards,
        mesh=mesh,
        in_specs=(
            P("seg", "bond", None, None),
            P("seg", None, None),
            P("seg", "bond", None, None),
            P("seg", None, None, "bond"),
            P("seg", None, None, None, None),
            P("seg", "bond", None, None),
            P("seg", None, None),
        ),
        out_specs=(P("seg", "bond", None, None), P("seg", "bond", None)),
        check_vma=False,
    )
```

profile of v0, /device:TPU:1, one launch (start us, length us, event | category | flops | bytes accessed | tf_op | source)
XLA Modules:
  0.0 756.7 jit_solution(14787921494383537855)
XLA Ops:
  8.0 2.2 copy.56
  11.0 3.0 collective-permute-start
  14.1 75.9 %all-gather.7.cloned.1.call-done = bf16[1,1024,4,1024]{3,2,0,1:T(4,128)(2,1)} async-done(((bf16[1,64,4,1024]{3,2,0,1:T(4,128)(2,1)}), bf16[1,1024,4,1024]{3,2,0,1:T(4,128)(2,1)}) %all-gather.7.cloned.1.call-update) | async-done | bytes 8388624 | tf_op jit(solution)/shard_map/all_gather | solution.py:22
  90.0 13.8 %copy.82 = bf16[1,1024,4,1024]{1,3,2,0:T(8,128)(2,1)} copy(bf16[1,1024,4,1024]{3,2,0,1:T(4,128)(2,1)} %all-gather.7.cloned.1.call-done) | data formatting | bytes 16777216 | tf_op jit(solution)/shard_map/reshape | solution.py:25
  103.9 64.7 %all-gather.11.cloned.1.call-done = bf16[1,1024,4,1024]{1,2,0,3:T(4,128)(2,1)} async-done(((bf16[1,1024,4,64]{1,2,0,3:T(4,128)(2,1)}), bf16[1,1024,4,1024]{1,2,0,3:T(4,128)(2,1)}) %all-gather.11.cloned.1.call-update) | async-done | bytes 8388624 | tf_op jit(solution)/shard_map/all_gather | solution.py:37
  168.6 13.7 %copy.57 = bf16[1,1024,4,1024]{3,1,2,0:T(8,128)(2,1)} copy(bf16[1,1024,4,1024]{1,2,0,3:T(4,128)(2,1)} %all-gather.11.cloned.1.call-done) | data formatting | bytes 16777216 | tf_op jit(solution)/shard_map/all_gather | solution.py:37
  182.3 6.3 fusion.14
  188.6 11.5 %fusion.8 = bf16[64,4,6,1024]{3,2,1,0:T(8,128)(2,1)} fusion(f32[64,6,4,1024,1]{3,0,2,1,4:T(8,128)S(1)} %fusion.14, bf16[1,6,6,4,4]{2,4,3,1,0:T(4,128)(2,1)S(1)} %copy-done.4), kind=kOutput, calls=%fused_computation.11 | convolution fusion | flops 454557696 | bytes 9438336 | tf_op jit(solution)/shard_map/autc,uvst->asvc/dot_general | solution.py:28
  200.2 65.7 %all-gather.9.cloned.1.call-done = bf16[1,1024,6,1024]{3,1,2,0:T(8,128)(2,1)} async-done(((bf16[1,64,6,1024]{3,1,2,0:T(8,128)(2,1)}), bf16[1,1024,6,1024]{3,1,2,0:T(8,128)(2,1)}) %all-gather.9.cloned.1.call-update) | async-done | bytes 12582928 | tf_op jit(solution)/shard_map/all_gather | solution.py:34
  265.9 12.8 %fusion.24 = f32[64,4,1024]{2,0,1:T(8,128)} fusion(bf16[1,1024,6,1024]{3,1,2,0:T(8,128)(2,1)} %all-gather.9.cloned.1.call-done, bf16[64,4,6,1024]{3,2,1,0:T(8,128)(2,1)} %fusion.8), kind=kOutput, calls=%fused_computation.23 | convolution fusion | flops 3221487616 | bytes 16777216 | tf_op jit(solution)/shard_map/asvc,cvy->asy/dot_general | solution.py:31
  278.7 5.8 fusion.29
  284.5 5.1 convolution_bitcast_fusion
  291.1 111.9 %all-reduce.3.cloned.1.call-done = f32[1024,1024]{0,1:T(8,128)} async-done(((f32[1024,1024]{0,1:T(8,128)}), f32[1024,1024]{0,1:T(8,128)}) %all-reduce.3.cloned.1.call-update) | async-done | bytes 4194320 | tf_op jit(solution)/shard_map/psum | solution.py:49
  403.0 5.5 copy.59
  408.5 4.4 fusion.9
  412.9 1.9 copy-done.2
  414.9 11.7 %cholesky.223 = f32[128,128]{1,0:T(8,128)S(1)} custom-call(f32[128,128]{1,0:T(8,128)S(1)} %cholesky.580), custom_call_target="Cholesky" | custom-call | tf_op jit(solution)/shard_map/jit(cholesky)/cholesky | solution.py:50
  426.6 9.8 %custom-call.63 = f32[1,128,128]{1,2,0:T(8,128)S(1)} custom-call(f32[1,128,128]{2,1,0:T(8,128)S(1)} %get-tuple-element.76), custom_call_target="InvertDiagBlocksLowerTriangular" | custom-call | tf_op jit(solution)/shard_map/jit(cholesky)/cholesky | solution.py:50
  436.4 1.6 fusion.53
  438.3 1.9 convolution_subtract_fusion
  440.2 2.5 cholesky.255
  442.7 11.9 %cholesky.244 = f32[128,128]{1,0:T(8,128)S(1)} custom-call(f32[128,128]{1,0:T(8,128)S(1)} %cholesky.584), custom_call_target="Cholesky" | custom-call | tf_op jit(solution)/shard_map/jit(cholesky)/cholesky | solution.py:50
  456.1 9.8 %custom-call.64 = f32[1,128,128]{1,2,0:T(8,128)S(1)} custom-call(f32[1,128,128]{2,1,0:T(8,128)S(1)} %get-tuple-element.73), custom_call_target="InvertDiagBlocksLowerTriangular" | custom-call | tf_op jit(solution)/shard_map/jit(cholesky)/cholesky | solution.py:50
  465.9 1.2 convolution_dynamic-update-slice_fusion
  467.2 2.1 convolution_subtract_fusion.1
  469.3 11.7 %cholesky.468 = f32[128,128]{1,0:T(8,128)S(1)} custom-call(f32[128,128]{1,0:T(8,128)S(1)} %cholesky.589), custom_call_target="Cholesky" | custom-call | tf_op jit(solution)/shard_map/jit(cholesky)/cholesky | solution.py:50
  482.3 9.8 %custom-call.65 = f32[1,128,128]{1,2,0:T(8,128)S(1)} custom-call(f32[1,128,128]{2,1,0:T(8,128)S(1)} %get-tuple-element.70), custom_call_target="InvertDiagBlocksLowerTriangular" | custom-call | tf_op jit(solution)/shard_map/jit(cholesky)/cholesky | solution.py:50
  492.1 1.2 convolution_dynamic-update-slice_fusion.1
  493.3 2.3 convolution_subtract_fusion.2
  495.6 12.1 %cholesky.487 = f32[128,128]{1,0:T(8,128)S(1)} custom-call(f32[128,128]{1,0:T(8,128)S(1)} %cholesky.594), custom_call_target="Cholesky" | custom-call | tf_op jit(solution)/shard_map/jit(cholesky)/cholesky | solution.py:50
  509.0 9.8 %custom-call.66 = f32[1,128,128]{1,2,0:T(8,128)S(1)} custom-call(f32[1,128,128]{2,1,0:T(8,128)S(1)} %get-tuple-element.67), custom_call_target="InvertDiagBlocksLowerTriangular" | custom-call | tf_op jit(solution)/shard_map/jit(cholesky)/cholesky | solution.py:50
  518.9 1.1 convolution_dynamic-update-slice_fusion.2
  520.0 2.3 convolution_subtract_fusion.3
  522.3 11.7 %cholesky.506 = f32[128,128]{1,0:T(8,128)S(1)} custom-call(f32[128,128]{1,0:T(8,128)S(1)} %cholesky.599), custom_call_target="Cholesky" | custom-call | tf_op jit(solution)/shard_map/jit(cholesky)/cholesky | solution.py:50
  535.4 10.0 %custom-call.67 = f32[1,128,128]{1,2,0:T(8,128)S(1)} custom-call(f32[1,128,128]{2,1,0:T(8,128)S(1)} %get-tuple-element.64), custom_call_target="InvertDiagBlocksLowerTriangular" | custom-call | tf_op jit(solution)/shard_map/jit(cholesky)/cholesky | solution.py:50
  546.4 2.3 convolution_subtract_fusion.4
  548.7 11.7 %cholesky.526 = f32[128,128]{1,0:T(8,128)S(1)} custom-call(f32[128,128]{1,0:T(8,128)S(1)} %cholesky.604), custom_call_target="Cholesky" | custom-call | tf_op jit(solution)/shard_map/jit(cholesky)/cholesky | solution.py:50
  561.7 9.8 %custom-call.68 = f32[1,128,128]{1,2,0:T(8,128)S(1)} custom-call(f32[1,128,128]{2,1,0:T(8,128)S(1)} %get-tuple-element.61), custom_call_target="InvertDiagBlocksLowerTriangular" | custom-call | tf_op jit(solution)/shard_map/jit(cholesky)/cholesky | solution.py:50
  572.4 2.0 convolution_subtract_fusion.11
  574.5 11.9 %cholesky.546 = f32[128,128]{1,0:T(8,128)S(1)} custom-call(f32[128,128]{1,0:T(8,128)S(1)} %cholesky.609), custom_call_target="Cholesky" | custom-call | tf_op jit(solution)/shard_map/jit(cholesky)/cholesky | solution.py:50
  587.6 9.8 %custom-call.69 = f32[1,128,128]{1,2,0:T(8,128)S(1)} custom-call(f32[1,128,128]{2,1,0:T(8,128)S(1)} %get-tuple-element.58), custom_call_target="InvertDiagBlocksLowerTriangular" | custom-call | tf_op jit(solution)/shard_map/jit(cholesky)/cholesky | solution.py:50
  598.3 1.8 convolution_subtract_fusion.13
  600.1 11.7 %cholesky.564 = f32[128,128]{1,0:T(8,128)S(1)} custom-call(f32[128,128]{1,0:T(8,128)S(1)} %convolution_subtract_fusion.13), custom_call_target="Cholesky" | custom-call | tf_op jit(solution)/shard_map/jit(cholesky)/cholesky | solution.py:50
  618.8 6.6 fusion.10
  625.3 27.4 %while.1 = (s32[]{:T(128)}, f32[1024,1024]{1,0:T(8,128)}, s32[8,2]{0,1:T(2,128)S(1)}, f32[8,128,128]{2,1,0:T(8,128)}, s32[]{:T(128)}) while((s32[]{:T(128)}, f32[1024,1024]{1,0:T(8,128)}, s32[8,2]{0,1:T(2,128)S(1)}, f32[8,128,128]{2,1,0:T(8,128)}, s32[]{:T(128)}) %tuple.65), condition=%wide.while_cond, body=%wide.while_body.sunk | while | flops 2 | bytes 132705 | solution.py:51
  625.9 2.8 bitcast_dynamic-update-slice_fusion.2
  629.4 2.8 bitcast_dynamic-update-slice_fusion.2
  632.8 2.8 bitcast_dynamic-update-slice_fusion.2
  636.2 2.8 bitcast_dynamic-update-slice_fusion.2
  639.6 2.8 bitcast_dynamic-update-slice_fusion.2
  643.1 2.8 bitcast_dynamic-update-slice_fusion.2
  646.5 2.8 bitcast_dynamic-update-slice_fusion.2
  649.9 2.8 bitcast_dynamic-update-slice_fusion.2
  652.7 79.6 %custom-call.70 = f32[8,128,128]{1,2,0:T(8,128)S(1)} custom-call(f32[8,128,128]{2,1,0:T(8,128)} %get-tuple-element.9), custom_call_target="InvertDiagBlocksLowerTriangular" | custom-call | tf_op jit(solution)/shard_map/jit(_solve_triangular)/triangular_solve | solution.py:51
  732.7 1.1 convolution_subtract_fusion.10
  734.1 1.2 convolution_subtract_fusion.8
  735.6 1.3 convolution_subtract_fusion.7
  737.3 1.4 convolution_subtract_fusion.6
  739.0 1.5 convolution_subtract_fusion.5
  740.8 1.7 convolution_subtract_fusion.9
  742.5 1.2 constant_dynamic-update-slice_fusion.11
  743.6 1.6 convolution_subtract_fusion.12
  745.3 1.2 convolution_dynamic-update-slice_fusion.4
  747.7 1.2 multiply_bitcast_fusion
  (79 shorter events, 25.0 us)
Async XLA Ops:
  7.2 271.5 %copy-start = (bf16[1,1024,1024]{2,1,0:T(8,128)(2,1)S(1)}, bf16[1,1024,1024]{2,1,0:T(8,128)(2,1)}, u32[]{:S(2)}) copy-start(bf16[1,1024,1024]{2,1,0:T(8,128)(2,1)} %param.13) | copy-start | bytes 6291460
  7.2 82.9 %all-gather.7.cloned.1.call-start = ((), (), s32[]{:S(2)}) async-start(), calls=%async_computation.1 | async-start | bytes 8912896 | tf_op jit(solution)/shard_map/all_gather | solution.py:22
  7.9 160.7 %all-gather.11.cloned.1.call-start = ((), (), s32[]{:S(2)}) async-start(), calls=%async_computation.3 | async-start | bytes 8912896 | tf_op jit(solution)/shard_map/all_gather | solution.py:37
  10.2 255.6 %all-gather.9.cloned.1.call-start = ((), (), s32[]{:S(2)}) async-start(), calls=%async_computation.2 | async-start | bytes 13369344 | tf_op jit(solution)/shard_map/all_gather | solution.py:34
  11.0 392.0 %all-reduce.3.cloned.1.call-start = ((), (), s32[]{:S(2)}) async-start(), calls=%async_computation | async-start | bytes 8388608 | tf_op jit(solution)/shard_map/psum | solution.py:49
  11.0 171.3 %collective-permute-start = (bf16[64,6,1024]{2,0,1:T(8,128)(2,1)}, bf16[64,6,1024]{2,0,1:T(8,128)(2,1)S(1)}, u32[]{:S(2)}, u32[]{:S(2)}) collective-permute-start(bf16[64,6,1024]{2,0,1:T(8,128)(2,1)} %bitcast.185), channel_id=1, source_target_pairs={{240,0},{0,16},{16,32},{32,48},{48,64},{64,80},{80,96},{96,112},{1... | collective-permute-start | bytes 2359304 | tf_op jit(solution)/shard_map/ppermute | solution.py:14
  14.1 264.6 %collective-permute-start.1 = (bf16[1024,1024]{1,0:T(8,128)(2,1)}, bf16[1024,1024]{1,0:T(8,128)(2,1)}, u32[]{:S(2)}, u32[]{:S(2)}) collective-permute-start(bf16[1024,1024]{1,0:T(8,128)(2,1)} %bitcast.184), channel_id=1, source_target_pairs={{240,0},{0,16},{16,32},{32,48},{48,64},{64,80},{80,96},{96,112},{1... | collective-permute-start | bytes 6291464 | tf_op jit(solution)/shard_map/ppermute | solution.py:14
  182.3 6.3 copy-start.4
  412.9 1.9 copy-start.2
  732.3 8.1 %copy-start.3 = (f32[8,128,128]{1,2,0:T(8,128)}, f32[8,128,128]{1,2,0:T(8,128)S(1)}, u32[]{:S(2)}) copy-start(f32[8,128,128]{1,2,0:T(8,128)S(1)} %custom-call.70) | copy-start | bytes 1572868
  740.8 9.1 %copy-start.1 = (bf16[1,1024,1024]{2,1,0:T(8,128)(2,1)S(1)}, bf16[1,1024,1024]{2,1,0:T(8,128)(2,1)}, u32[]{:S(2)}) copy-start(bf16[1,1024,1024]{2,1,0:T(8,128)(2,1)} %param.13) | copy-start | bytes 6291460
Sparse Core Ops, SparseCore 0:
  10.4 79.5 all-gather.6
  93.0 75.4 all-gather.10
  171.1 94.7 all-gather.8
  289.8 113.1 all-reduce.2
where the time goes:
time: 764 us; the launch traced here: 757 us
  waiting for transfers between devices  320 us (42%)
  other arithmetic  264 us (35%)
  matrix products  78.2 us (10%)
  local copies, waits for them, and re-layouts  71.6 us (9%)
  between operations  19.4 us (3%)
    another operation x30, other arithmetic, shards(): triangle = jnp.linalg.cholesky(correlation)  172 us
    psum x1, waiting for transfers between devices, shards(): correlation = lax.psum(local_correlation, 'bond')  112 us
    another operation x3, other arithmetic, shards(): solved = jax.scipy.linalg.solve_triangular(triangle, target.T, lower=True)  86.2 us
    all_gather x1, waiting for transfers between devices, shards(): current = lax.all_gather(cur_site[0], 'bond', axis=0, tiled=True)  75.9 us
    all_gather x1, waiting for transfers between devices, shards(): lax.all_gather(right_env[0], 'bond', axis=0, tiled=True)  65.7 us
    all_gather x1, waiting for transfers between devices, shards(): previous = lax.all_gather(prev_site[0], 'bond', axis=2, tiled=True)  64.7 us
    another operation x24, local copies, waits for them, and re-layouts  27.4 us
    another operation x14, matrix products, shards(): triangle = jnp.linalg.cholesky(correlation)  22.7 us
  transfers between devices with their start and end apart: 6, of which 4 were waited for; matrix products, arithmetic and copies ran while one was open for 8% of the time, Pallas kernels for 0%

commit v1 on v0

--- a/solution.py
+++ b/solution.py
@@ -6,6 +6,31 @@
 
 PHYS = 4
 MPOB = 6
+
+
+def in_order(blocks, dim):
+    shape = list(blocks.shape[1:])
+    shape[dim] *= blocks.shape[0]
+    return jnp.moveaxis(blocks, 0, dim).reshape(shape)
+
+
+def work_both_ways(x, axis, dim, apply, out_dim):
+    size, index, width = (lax.axis_size(axis), lax.axis_index(axis), x.shape[dim])
+    forward = [(i, (i + 1) % size) for i in range(size)]
+    backward = [(i, (i - 1) % size) for i in range(size)]
+    halfway = size // 2
+    tiles = {}
+    from_left = from_right = x
+    for step in range(halfway + 1):
+        next_left = lax.ppermute(from_left, axis, forward) if step < halfway else None
+        next_right = lax.ppermute(from_right, axis, backward) if step < size - halfway - 1 else None
+        tiles[-step] = apply(from_left, (index - step) % size * width)
+        if 0 < step < size - halfway:
+            tiles[step] = apply(from_right, (index + step) % size * width)
+        from_left, from_right = (next_left, next_right)
+    tiles = jnp.stack([tiles[k] for k in sorted(tiles)])
+    tiles = tiles[(jnp.arange(size) - index + halfway) % size]
+    return in_order(tiles, out_dim)
 
 
 def shifted(block, axis, distance):
@@ -34,10 +59,15 @@
         lax.all_gather(right_env[0], "bond", axis=0, tiled=True),
         preferred_element_type=jnp.float32,
     )
-    previous = lax.all_gather(prev_site[0], "bond", axis=2, tiled=True)
     own_left = lax.dynamic_slice_in_dim(prev_now, lax.axis_index("bond") * own_rows, own_rows, 0)
-    partial_value = jnp.einsum(
-        "ab,bsc->asc", own_left, previous, preferred_element_type=jnp.float32
+    partial_value = work_both_ways(
+        prev_site[0],
+        "bond",
+        2,
+        lambda part, offset_2: jnp.einsum(
+            "ab,bsc->asc", own_left, part, preferred_element_type=jnp.float32
+        ),
+        2,
     ).astype(jnp.bfloat16)
     second = jnp.einsum(
         "asc,cy->asy", partial_value, prev_right[0], preferred_element_type=jnp.float32

time: 764 us -> 740 us (0.969)
  waiting for transfers between devices: 320 us -> 182 us
  starting transfers between devices: 3.24 us -> 97.1 us
  matrix products: 78.2 us -> 104 us
  local copies, waits for them, and re-layouts: 71.6 us -> 62.8 us
    all_gather x1, waiting for transfers between devices: 75.9 us -> 0.01 us  [shards(): current = lax.all_gather(cur_site[0], 'bond', axis=0, tiled=True)]
    ppermute x0 -> x15, waiting for transfers between devices: none -> 66.4 us  [the longest x8 40.9 us: work_both_ways(): lax.ppermute(from_left, axis, forward)]
    all_gather x1, waiting for transfers between devices: 65.7 us -> 0.01 us  [shards(): lax.all_gather(right_env[0], 'bond', axis=0, tiled=True)]
    all_gather x1 -> x0, waiting for transfers between devices: 64.7 us -> none  [shards(): previous = lax.all_gather(prev_site[0], 'bond', axis=2, tiled=True)]
    ppermute x2, starting transfers between devices: 3.08 us -> 58.2 us  [shifted(): return lax.ppermute(block, axis, route)]
    ppermute x0 -> x15, starting transfers between devices: none -> 38.8 us  [the longest x7 36.5 us: work_both_ways(): lax.ppermute(from_right, axis, backward)]
    dot_general x0 -> x16, matrix products: none -> 32.2 us  [shards(): jnp.einsum('ab,bsc->asc', own_left, part, preferred_element_type=jnp.floa...]
    all_gather x1 -> x0, local copies, waits for them, and re-layouts: 13.7 us -> none  [shards(): previous = lax.all_gather(prev_site[0], 'bond', axis=2, tiled=True)]
  transfers between devices with their start and end apart: 6 -> 20, of which waited for: 4 -> 9; matrix products, arithmetic and copies ran while one was open for 8% -> 10% of each run, Pallas kernels for 0% -> 0%
where the time goes in v1:
time: 740 us; the launch traced here: 730 us
  other arithmetic  265 us (36%)
  waiting for transfers between devices  182 us (25%)
  matrix products  104 us (14%)
  starting transfers between devices  97.1 us (13%)
  local copies, waits for them, and re-layouts  62.8 us (8%)
  between operations  19.6 us (3%)
    another operation x30, other arithmetic, shards(): triangle = jnp.linalg.cholesky(correlation)  173 us
    psum x1, waiting for transfers between devices, shards(): correlation = lax.psum(local_correlation, 'bond')  114 us
    another operation x3, other arithmetic, shards(): solved = jax.scipy.linalg.solve_triangular(triangle, target.T, lower=True)  86.2 us
    ppermute x2, starting transfers between devices, shifted(): return lax.ppermute(block, axis, route)  58.2 us
    ppermute x8, waiting for transfers between devices, work_both_ways(): lax.ppermute(from_left, axis, forward)  40.9 us
    ppermute x7, starting transfers between devices, work_both_ways(): lax.ppermute(from_right, axis, backward)  36.5 us
    dot_general x16, matrix products, shards(): jnp.einsum('ab,bsc->asc', own_left, part, preferred_element_type=jnp.floa...  32.2 us
    another operation x24, local copies, waits for them, and re-layouts  27.3 us
  transfers between devices with their start and end apart: 20, of which 9 were waited for; matrix products, arithmetic and copies ran while one was open for 10% of the time, Pallas kernels for 0%

profile of v1, /device:TPU:1, one launch (start us, length us, event | category | flops | bytes accessed | tf_op | source)
XLA Modules:
  0.0 729.9 jit_solution(16306014919667298672)
XLA Ops:
  8.7 2.2 collective-permute-start.2
  10.9 13.5 %collective-permute-done.2 = bf16[1024,4,64]{0,2,1:T(8,128)(2,1)S(1)} collective-permute-done((bf16[1024,4,64]{0,2,1:T(8,128)(2,1)}, bf16[1024,4,64]{0,2,1:T(8,128)(2,1)S(1)}, u32[]{:S(2)}, u32[]{:S(2)}) %collective-permute-start.2) | collective-permute-done | bytes 524320 | tf_op jit(solution)/shard_map/ppermute | solution.py:25
  24.5 4.8 collective-permute-start.10
  29.2 15.1 %collective-permute-done.3 = bf16[1024,4,64]{0,2,1:T(8,128)(2,1)S(1)} collective-permute-done((bf16[1024,4,64]{0,2,1:T(8,128)(2,1)S(1)}, bf16[1024,4,64]{0,2,1:T(8,128)(2,1)S(1)}, u32[]{:S(2)}, u32[]{:S(2)}) %collective-permute-start.3) | collective-permute-done | bytes 524320 | tf_op jit(solution)/shard_map/ppermute | solution.py:25
  45.2 5.2 collective-permute-start.11
  50.4 5.3 collective-permute-done.4
  56.5 5.2 collective-permute-start.12
  61.8 6.3 collective-permute-done.5
  68.0 31.2 %collective-permute-start.1 = (bf16[1024,1024]{1,0:T(8,128)(2,1)}, bf16[1024,1024]{1,0:T(8,128)(2,1)}, u32[]{:S(2)}, u32[]{:S(2)}) collective-permute-start(bf16[1024,1024]{1,0:T(8,128)(2,1)} %bitcast.301), channel_id=1, source_target_pairs={{240,0},{0,16},{16,32},{32,48},{48,64},{64,80},{80,96},{96,112},{1... | collective-permute-start | bytes 6291464 | tf_op jit(solution)/shard_map/ppermute | solution.py:39
  99.3 5.1 collective-permute-start.13
  104.5 14.7 %collective-permute-done.13 = bf16[1024,4,64]{0,2,1:T(8,128)(2,1)S(1)} collective-permute-done((bf16[1024,4,64]{0,2,1:T(8,128)(2,1)S(1)}, bf16[1024,4,64]{0,2,1:T(8,128)(2,1)S(1)}, u32[]{:S(2)}, u32[]{:S(2)}) %collective-permute-start.13) | collective-permute-done | bytes 524320 | tf_op jit(solution)/shard_map/ppermute | solution.py:26
  119.2 5.3 collective-permute-start.14
  125.1 10.0 %collective-permute-done.14 = bf16[1024,4,64]{0,2,1:T(8,128)(2,1)} collective-permute-done((bf16[1024,4,64]{0,2,1:T(8,128)(2,1)S(1)}, bf16[1024,4,64]{0,2,1:T(8,128)(2,1)}, u32[]{:S(2)}, u32[]{:S(2)}) %collective-permute-start.14) | collective-permute-done | bytes 524320 | tf_op jit(solution)/shard_map/ppermute | solution.py:26
  135.1 5.3 collective-permute-start.15
  140.4 26.9 %collective-permute-start = (bf16[64,6,1024]{2,0,1:T(8,128)(2,1)}, bf16[64,6,1024]{2,0,1:T(8,128)(2,1)}, u32[]{:S(2)}, u32[]{:S(2)}) collective-permute-start(bf16[64,6,1024]{2,0,1:T(8,128)(2,1)} %bitcast.302), channel_id=1, source_target_pairs={{240,0},{0,16},{16,32},{32,48},{48,64},{64,80},{80,96},{96,112},{1... | collective-permute-start | bytes 2359304 | tf_op jit(solution)/shard_map/ppermute | solution.py:39
  167.4 5.6 collective-permute-start.16
  173.0 2.1 fusion.45
  175.2 2.2 fusion.44
  177.3 2.1 fusion.43
  179.4 2.2 fusion.42
  181.6 2.2 fusion.41
  183.7 2.1 fusion.40
  199.2 2.1 fusion.32
  201.3 2.1 fusion.31
  209.0 2.6 convert_element_type.26
  211.6 13.9 %copy.63 = bf16[1,1024,4,1024]{1,3,2,0:T(8,128)(2,1)} copy(bf16[1,1024,4,1024]{3,2,0,1:T(4,128)(2,1)} %all-gather.5.cloned.1.call-done) | data formatting | bytes 16777216 | tf_op jit(solution)/shard_map/reshape | solution.py:50
  225.5 6.1 fusion.12
  231.6 11.0 %fusion.6 = bf16[64,4,6,1024]{3,2,1,0:T(8,128)(2,1)} fusion(f32[64,6,4,1024,1]{3,0,2,1,4:T(8,128)S(1)} %fusion.12, bf16[1,6,6,4,4]{2,4,3,1,0:T(4,128)(2,1)S(1)} %copy-done.20), kind=kOutput, calls=%fused_computation.10 | convolution fusion | flops 454557696 | bytes 9438336 | tf_op jit(solution)/shard_map/autc,uvst->asvc/dot_general | solution.py:53
  242.6 11.6 %fusion.22 = f32[64,4,1024]{2,0,1:T(8,128)S(1)} fusion(bf16[1,1024,6,1024]{3,1,2,0:T(8,128)(2,1)} %all-gather.7.cloned.1.call-done, bf16[64,4,6,1024]{3,2,1,0:T(8,128)(2,1)} %fusion.6), kind=kOutput, calls=%fused_computation.22 | convolution fusion | flops 3221487616 | bytes 16777216 | tf_op jit(solution)/shard_map/asvc,cvy->asy/dot_general | solution.py:56
  255.0 5.3 convolution_bitcast_fusion
  261.8 114.1 %all-reduce.3.cloned.1.call-done = f32[1024,1024]{0,1:T(8,128)} async-done(((f32[1024,1024]{0,1:T(8,128)}), f32[1024,1024]{0,1:T(8,128)}) %all-reduce.3.cloned.1.call-update) | async-done | bytes 4194320 | tf_op jit(solution)/shard_map/psum | solution.py:79
  375.9 5.4 copy.40
  381.3 4.4 fusion.7
  387.7 11.7 %cholesky.223 = f32[128,128]{1,0:T(8,128)S(1)} custom-call(f32[128,128]{1,0:T(8,128)S(1)} %cholesky.580), custom_call_target="Cholesky" | custom-call | tf_op jit(solution)/shard_map/jit(cholesky)/cholesky | solution.py:80
  399.5 9.8 %custom-call.63 = f32[1,128,128]{1,2,0:T(8,128)S(1)} custom-call(f32[1,128,128]{2,1,0:T(8,128)S(1)} %get-tuple-element.74), custom_call_target="InvertDiagBlocksLowerTriangular" | custom-call | tf_op jit(solution)/shard_map/jit(cholesky)/cholesky | solution.py:80
  413.0 2.5 cholesky.255
  415.5 12.1 %cholesky.244 = f32[128,128]{1,0:T(8,128)S(1)} custom-call(f32[128,128]{1,0:T(8,128)S(1)} %cholesky.584), custom_call_target="Cholesky" | custom-call | tf_op jit(solution)/shard_map/jit(cholesky)/cholesky | solution.py:80
  429.1 9.8 %custom-call.64 = f32[1,128,128]{1,2,0:T(8,128)S(1)} custom-call(f32[1,128,128]{2,1,0:T(8,128)S(1)} %get-tuple-element.71), custom_call_target="InvertDiagBlocksLowerTriangular" | custom-call | tf_op jit(solution)/shard_map/jit(cholesky)/cholesky | solution.py:80
  440.2 2.1 convolution_subtract_fusion.1
  442.3 11.7 %cholesky.468 = f32[128,128]{1,0:T(8,128)S(1)} custom-call(f32[128,128]{1,0:T(8,128)S(1)} %cholesky.589), custom_call_target="Cholesky" | custom-call | tf_op jit(solution)/shard_map/jit(cholesky)/cholesky | solution.py:80
  455.3 9.8 %custom-call.65 = f32[1,128,128]{1,2,0:T(8,128)S(1)} custom-call(f32[1,128,128]{2,1,0:T(8,128)S(1)} %get-tuple-element.68), custom_call_target="InvertDiagBlocksLowerTriangular" | custom-call | tf_op jit(solution)/shard_map/jit(cholesky)/cholesky | solution.py:80
  466.3 2.3 convolution_subtract_fusion.2
  468.7 11.9 %cholesky.487 = f32[128,128]{1,0:T(8,128)S(1)} custom-call(f32[128,128]{1,0:T(8,128)S(1)} %cholesky.594), custom_call_target="Cholesky" | custom-call | tf_op jit(solution)/shard_map/jit(cholesky)/cholesky | solution.py:80
  481.9 9.8 %custom-call.66 = f32[1,128,128]{1,2,0:T(8,128)S(1)} custom-call(f32[1,128,128]{2,1,0:T(8,128)S(1)} %get-tuple-element.65), custom_call_target="InvertDiagBlocksLowerTriangular" | custom-call | tf_op jit(solution)/shard_map/jit(cholesky)/cholesky | solution.py:80
  492.8 2.3 convolution_subtract_fusion.3
  495.2 11.7 %cholesky.506 = f32[128,128]{1,0:T(8,128)S(1)} custom-call(f32[128,128]{1,0:T(8,128)S(1)} %cholesky.599), custom_call_target="Cholesky" | custom-call | tf_op jit(solution)/shard_map/jit(cholesky)/cholesky | solution.py:80
  508.2 10.0 %custom-call.67 = f32[1,128,128]{1,2,0:T(8,128)S(1)} custom-call(f32[1,128,128]{2,1,0:T(8,128)S(1)} %get-tuple-element.62), custom_call_target="InvertDiagBlocksLowerTriangular" | custom-call | tf_op jit(solution)/shard_map/jit(cholesky)/cholesky | solution.py:80
  519.2 2.3 convolution_subtract_fusion.4
  521.5 11.7 %cholesky.526 = f32[128,128]{1,0:T(8,128)S(1)} custom-call(f32[128,128]{1,0:T(8,128)S(1)} %cholesky.604), custom_call_target="Cholesky" | custom-call | tf_op jit(solution)/shard_map/jit(cholesky)/cholesky | solution.py:80
  534.5 9.8 %custom-call.68 = f32[1,128,128]{1,2,0:T(8,128)S(1)} custom-call(f32[1,128,128]{2,1,0:T(8,128)S(1)} %get-tuple-element.59), custom_call_target="InvertDiagBlocksLowerTriangular" | custom-call | tf_op jit(solution)/shard_map/jit(cholesky)/cholesky | solution.py:80
  547.3 12.1 %cholesky.546 = f32[128,128]{1,0:T(8,128)S(1)} custom-call(f32[128,128]{1,0:T(8,128)S(1)} %cholesky.609), custom_call_target="Cholesky" | custom-call | tf_op jit(solution)/shard_map/jit(cholesky)/cholesky | solution.py:80
  560.7 9.8 %custom-call.69 = f32[1,128,128]{1,2,0:T(8,128)S(1)} custom-call(f32[1,128,128]{2,1,0:T(8,128)S(1)} %get-tuple-element.56), custom_call_target="InvertDiagBlocksLowerTriangular" | custom-call | tf_op jit(solution)/shard_map/jit(cholesky)/cholesky | solution.py:80
  573.2 11.7 %cholesky.564 = f32[128,128]{1,0:T(8,128)S(1)} custom-call(f32[128,128]{1,0:T(8,128)S(1)} %convolution_subtract_fusion.13), custom_call_target="Cholesky" | custom-call | tf_op jit(solution)/shard_map/jit(cholesky)/cholesky | solution.py:80
  592.1 6.6 fusion.8
  598.7 27.4 %while.1 = (s32[]{:T(128)}, f32[1024,1024]{1,0:T(8,128)}, s32[8,2]{0,1:T(2,128)S(1)}, f32[8,128,128]{2,1,0:T(8,128)}, s32[]{:T(128)}) while((s32[]{:T(128)}, f32[1024,1024]{1,0:T(8,128)}, s32[8,2]{0,1:T(2,128)S(1)}, f32[8,128,128]{2,1,0:T(8,128)}, s32[]{:T(128)}) %tuple.64), condition=%wide.while_cond, body=%wide.while_body.sunk | while | flops 2 | bytes 132705 | solution.py:81
  599.4 2.8 bitcast_dynamic-update-slice_fusion.2
  602.8 2.8 bitcast_dynamic-update-slice_fusion.2
  606.2 2.8 bitcast_dynamic-update-slice_fusion.2
  609.6 2.8 bitcast_dynamic-update-slice_fusion.2
  613.1 2.8 bitcast_dynamic-update-slice_fusion.2
  616.5 2.8 bitcast_dynamic-update-slice_fusion.2
  619.9 2.8 bitcast_dynamic-update-slice_fusion.2
  623.3 2.8 bitcast_dynamic-update-slice_fusion.2
  626.1 79.6 %custom-call.70 = f32[8,128,128]{1,2,0:T(8,128)S(1)} custom-call(f32[8,128,128]{2,1,0:T(8,128)} %get-tuple-element.9), custom_call_target="InvertDiagBlocksLowerTriangular" | custom-call | tf_op jit(solution)/shard_map/jit(_solve_triangular)/triangular_solve | solution.py:81
  (157 shorter events, 73.2 us)
Async XLA Ops:
  7.2 247.1 %copy-start = (bf16[1,1024,1024]{2,1,0:T(8,128)(2,1)S(1)}, bf16[1,1024,1024]{2,1,0:T(8,128)(2,1)}, u32[]{:S(2)}) copy-start(bf16[1,1024,1024]{2,1,0:T(8,128)(2,1)} %param.13) | copy-start | bytes 6291460
  7.2 182.5 %copy-start.4 = (bf16[1,1024,4,64]{1,3,2,0:T(8,128)(2,1)S(1)}, bf16[1,1024,4,64]{1,3,2,0:T(8,128)(2,1)}, u32[]{:S(2)}) copy-start(bf16[1,1024,4,64]{1,3,2,0:T(8,128)(2,1)} %param.10) | copy-start | bytes 1572868
  7.2 204.4 %all-gather.5.cloned.1.call-start = ((), (), s32[]{:S(2)}) async-start(), calls=%async_computation.1 | async-start | bytes 8912896 | tf_op jit(solution)/shard_map/all_gather | solution.py:47
  7.9 234.7 %all-gather.7.cloned.1.call-start = ((), (), s32[]{:S(2)}) async-start(), calls=%async_computation.2 | async-start | bytes 13369344 | tf_op jit(solution)/shard_map/all_gather | solution.py:59
  8.7 367.3 %all-reduce.3.cloned.1.call-start = ((), (), s32[]{:S(2)}) async-start(), calls=%async_computation | async-start | bytes 8388608 | tf_op jit(solution)/shard_map/psum | solution.py:79
  8.7 15.7 %collective-permute-start.2 = (bf16[1024,4,64]{0,2,1:T(8,128)(2,1)}, bf16[1024,4,64]{0,2,1:T(8,128)(2,1)S(1)}, u32[]{:S(2)}, u32[]{:S(2)}) collective-permute-start(bf16[1024,4,64]{0,2,1:T(8,128)(2,1)} %bitcast.298), channel_id=1, source_target_pairs={{0,1},{1,2},{2,3},{3,4},{4,5},{5,6},{6,7},{7,8},{8,9},{9,10},{10,1... | collective-permute-start | bytes 1572872 | tf_op jit(solution)/shard_map/ppermute | solution.py:25
  24.5 19.9 %collective-permute-start.3 = (bf16[1024,4,64]{0,2,1:T(8,128)(2,1)S(1)}, bf16[1024,4,64]{0,2,1:T(8,128)(2,1)S(1)}, u32[]{:S(2)}, u32[]{:S(2)}) collective-permute-start(bf16[1024,4,64]{0,2,1:T(8,128)(2,1)S(1)} %collective-permute-done.2), channel_id=1, source_target_pairs={{0,1},{1,2},{2,3},{3,4},{4,5},{5,6},{6,7},{7,8},{8,9},{9,10},{10,1... | collective-permute-start | bytes 1572872 | tf_op jit(solution)/shard_map/ppermute | solution.py:25
  24.5 19.9 %collective-permute-start.10 = (bf16[1024,4,64]{0,2,1:T(8,128)(2,1)}, bf16[1024,4,64]{0,2,1:T(8,128)(2,1)S(1)}, u32[]{:S(2)}, u32[]{:S(2)}) collective-permute-start(bf16[1024,4,64]{0,2,1:T(8,128)(2,1)} %bitcast.299), channel_id=1, source_target_pairs={{0,15},{1,0},{2,1},{3,2},{4,3},{5,4},{6,5},{7,6},{8,7},{9,8},{10,9... | collective-permute-start | bytes 1572872 | tf_op jit(solution)/shard_map/ppermute | solution.py:26
  44.4 12.1 %copy-start.7 = (bf16[1024,4,64]{0,2,1:T(8,128)(2,1)}, bf16[1024,4,64]{0,2,1:T(8,128)(2,1)S(1)}, u32[]{:S(2)}) copy-start(bf16[1024,4,64]{0,2,1:T(8,128)(2,1)S(1)} %collective-permute-done.3) | copy-start | bytes 1572868
  44.4 11.4 %collective-permute-start.4 = (bf16[1024,4,64]{0,2,1:T(8,128)(2,1)S(1)}, bf16[1024,4,64]{0,2,1:T(8,128)(2,1)S(1)}, u32[]{:S(2)}, u32[]{:S(2)}) collective-permute-start(bf16[1024,4,64]{0,2,1:T(8,128)(2,1)S(1)} %collective-permute-done.3), channel_id=1, source_target_pairs={{0,1},{1,2},{2,3},{3,4},{4,5},{5,6},{6,7},{7,8},{8,9},{9,10},{10,1... | collective-permute-start | bytes 1572872 | tf_op jit(solution)/shard_map/ppermute | solution.py:25
  44.4 0.8 copy-start.5
  45.2 11.3 %collective-permute-start.11 = (bf16[1024,4,64]{0,2,1:T(8,128)(2,1)S(1)}, bf16[1024,4,64]{0,2,1:T(8,128)(2,1)S(1)}, u32[]{:S(2)}, u32[]{:S(2)}) collective-permute-start(bf16[1024,4,64]{0,2,1:T(8,128)(2,1)S(1)} %collective-permute-done.10), channel_id=1, source_target_pairs={{0,15},{1,0},{2,1},{3,2},{4,3},{5,4},{6,5},{7,6},{8,7},{9,8},{10,9... | collective-permute-start | bytes 1572872 | tf_op jit(solution)/shard_map/ppermute | solution.py:26
  55.7 43.5 %copy-start.11 = (bf16[1024,4,64]{0,2,1:T(8,128)(2,1)}, bf16[1024,4,64]{0,2,1:T(8,128)(2,1)S(1)}, u32[]{:S(2)}) copy-start(bf16[1024,4,64]{0,2,1:T(8,128)(2,1)S(1)} %collective-permute-done.4) | copy-start | bytes 1572868
  55.7 12.3 %collective-permute-start.5 = (bf16[1024,4,64]{0,2,1:T(8,128)(2,1)S(1)}, bf16[1024,4,64]{0,2,1:T(8,128)(2,1)S(1)}, u32[]{:S(2)}, u32[]{:S(2)}) collective-permute-start(bf16[1024,4,64]{0,2,1:T(8,128)(2,1)S(1)} %collective-permute-done.4), channel_id=1, source_target_pairs={{0,1},{1,2},{2,3},{3,4},{4,5},{5,6},{6,7},{7,8},{8,9},{9,10},{10,1... | collective-permute-start | bytes 1572872 | tf_op jit(solution)/shard_map/ppermute | solution.py:25
  56.5 5.2 copy-start.9
  56.5 42.7 %collective-permute-start.12 = (bf16[1024,4,64]{0,2,1:T(8,128)(2,1)S(1)}, bf16[1024,4,64]{0,2,1:T(8,128)(2,1)S(1)}, u32[]{:S(2)}, u32[]{:S(2)}) collective-permute-start(bf16[1024,4,64]{0,2,1:T(8,128)(2,1)S(1)} %collective-permute-done.11), channel_id=1, source_target_pairs={{0,15},{1,0},{2,1},{3,2},{4,3},{5,4},{6,5},{7,6},{8,7},{9,8},{10,9... | collective-permute-start | bytes 1572872 | tf_op jit(solution)/shard_map/ppermute | solution.py:26
  68.0 51.2 %copy-start.14 = (bf16[1024,4,64]{0,2,1:T(8,128)(2,1)}, bf16[1024,4,64]{0,2,1:T(8,128)(2,1)S(1)}, u32[]{:S(2)}) copy-start(bf16[1024,4,64]{0,2,1:T(8,128)(2,1)S(1)} %collective-permute-done.5) | copy-start | bytes 1572868
  68.0 36.4 %collective-permute-start.6 = (bf16[1024,4,64]{0,2,1:T(8,128)(2,1)S(1)}, bf16[1024,4,64]{0,2,1:T(8,128)(2,1)S(1)}, u32[]{:S(2)}, u32[]{:S(2)}) collective-permute-start(bf16[1024,4,64]{0,2,1:T(8,128)(2,1)S(1)} %collective-permute-done.5), channel_id=1, source_target_pairs={{0,1},{1,2},{2,3},{3,4},{4,5},{5,6},{6,7},{7,8},{8,9},{9,10},{10,1... | collective-permute-start | bytes 1572872 | tf_op jit(solution)/shard_map/ppermute | solution.py:25
  68.0 105.0 %collective-permute-start.1 = (bf16[1024,1024]{1,0:T(8,128)(2,1)}, bf16[1024,1024]{1,0:T(8,128)(2,1)}, u32[]{:S(2)}, u32[]{:S(2)}) collective-permute-start(bf16[1024,1024]{1,0:T(8,128)(2,1)} %bitcast.301), channel_id=1, source_target_pairs={{240,0},{0,16},{16,32},{32,48},{48,64},{64,80},{80,96},{96,112},{1... | collective-permute-start | bytes 6291464 | tf_op jit(solution)/shard_map/ppermute | solution.py:39
  99.3 5.1 copy-start.12
  99.3 19.9 %collective-permute-start.13 = (bf16[1024,4,64]{0,2,1:T(8,128)(2,1)S(1)}, bf16[1024,4,64]{0,2,1:T(8,128)(2,1)S(1)}, u32[]{:S(2)}, u32[]{:S(2)}) collective-permute-start(bf16[1024,4,64]{0,2,1:T(8,128)(2,1)S(1)} %collective-permute-done.12), channel_id=1, source_target_pairs={{0,15},{1,0},{2,1},{3,2},{4,3},{5,4},{6,5},{7,6},{8,7},{9,8},{10,9... | collective-permute-start | bytes 1572872 | tf_op jit(solution)/shard_map/ppermute | solution.py:26
  104.4 30.7 %copy-start.17 = (bf16[1024,4,64]{0,2,1:T(8,128)(2,1)}, bf16[1024,4,64]{0,2,1:T(8,128)(2,1)S(1)}, u32[]{:S(2)}) copy-start(bf16[1024,4,64]{0,2,1:T(8,128)(2,1)S(1)} %collective-permute-done.6) | copy-start | bytes 1572868
  104.4 20.7 %collective-permute-start.7 = (bf16[1024,4,64]{0,2,1:T(8,128)(2,1)S(1)}, bf16[1024,4,64]{0,2,1:T(8,128)(2,1)S(1)}, u32[]{:S(2)}, u32[]{:S(2)}) collective-permute-start(bf16[1024,4,64]{0,2,1:T(8,128)(2,1)S(1)} %collective-permute-done.6), channel_id=1, source_target_pairs={{0,1},{1,2},{2,3},{3,4},{4,5},{5,6},{6,7},{7,8},{8,9},{9,10},{10,1... | collective-permute-start | bytes 1572872 | tf_op jit(solution)/shard_map/ppermute | solution.py:25
  119.2 5.3 copy-start.15
  119.2 15.9 %collective-permute-start.14 = (bf16[1024,4,64]{0,2,1:T(8,128)(2,1)S(1)}, bf16[1024,4,64]{0,2,1:T(8,128)(2,1)}, u32[]{:S(2)}, u32[]{:S(2)}) collective-permute-start(bf16[1024,4,64]{0,2,1:T(8,128)(2,1)S(1)} %collective-permute-done.13), channel_id=1, source_target_pairs={{0,15},{1,0},{2,1},{3,2},{4,3},{5,4},{6,5},{7,6},{8,7},{9,8},{10,9... | collective-permute-start | bytes 1572872 | tf_op jit(solution)/shard_map/ppermute | solution.py:26
  125.1 15.4 %copy-start.18 = (bf16[1024,4,64]{0,2,1:T(8,128)(2,1)}, bf16[1024,4,64]{0,2,1:T(8,128)(2,1)S(1)}, u32[]{:S(2)}) copy-start(bf16[1024,4,64]{0,2,1:T(8,128)(2,1)S(1)} %collective-permute-done.7) | copy-start | bytes 1572868
  125.1 15.4 %collective-permute-start.8 = (bf16[1024,4,64]{0,2,1:T(8,128)(2,1)S(1)}, bf16[1024,4,64]{0,2,1:T(8,128)(2,1)}, u32[]{:S(2)}, u32[]{:S(2)}) collective-permute-start(bf16[1024,4,64]{0,2,1:T(8,128)(2,1)S(1)} %collective-permute-done.7), channel_id=1, source_target_pairs={{0,1},{1,2},{2,3},{3,4},{4,5},{5,6},{6,7},{7,8},{8,9},{9,10},{10,1... | collective-permute-start | bytes 1572872 | tf_op jit(solution)/shard_map/ppermute | solution.py:25
  135.1 32.3 %collective-permute-start.15 = (bf16[1024,4,64]{0,2,1:T(8,128)(2,1)}, bf16[1024,4,64]{0,2,1:T(8,128)(2,1)}, u32[]{:S(2)}, u32[]{:S(2)}) collective-permute-start(bf16[1024,4,64]{0,2,1:T(8,128)(2,1)} %collective-permute-done.14), channel_id=1, source_target_pairs={{0,15},{1,0},{2,1},{3,2},{4,3},{5,4},{6,5},{7,6},{8,7},{9,8},{10,9... | collective-permute-start | bytes 1572872 | tf_op jit(solution)/shard_map/ppermute | solution.py:26
  140.4 32.6 %collective-permute-start.9 = (bf16[1024,4,64]{0,2,1:T(8,128)(2,1)}, bf16[1024,4,64]{0,2,1:T(8,128)(2,1)}, u32[]{:S(2)}, u32[]{:S(2)}) collective-permute-start(bf16[1024,4,64]{0,2,1:T(8,128)(2,1)} %collective-permute-done.8), channel_id=1, source_target_pairs={{0,1},{1,2},{2,3},{3,4},{4,5},{5,6},{6,7},{7,8},{8,9},{9,10},{10,1... | collective-permute-start | bytes 1572872 | tf_op jit(solution)/shard_map/ppermute | solution.py:25
  140.4 85.1 %collective-permute-start = (bf16[64,6,1024]{2,0,1:T(8,128)(2,1)}, bf16[64,6,1024]{2,0,1:T(8,128)(2,1)}, u32[]{:S(2)}, u32[]{:S(2)}) collective-permute-start(bf16[64,6,1024]{2,0,1:T(8,128)(2,1)} %bitcast.302), channel_id=1, source_target_pairs={{240,0},{0,16},{16,32},{32,48},{48,64},{64,80},{80,96},{96,112},{1... | collective-permute-start | bytes 2359304 | tf_op jit(solution)/shard_map/ppermute | solution.py:39
  167.4 18.5 %copy-start.8 = (bf16[1024,4,64]{0,2,1:T(8,128)(2,1)S(1)}, bf16[1024,4,64]{0,2,1:T(8,128)(2,1)}, u32[]{:S(2)}) copy-start(bf16[1024,4,64]{0,2,1:T(8,128)(2,1)} %copy-done.7) | copy-start | bytes 1572868
  167.4 24.2 %copy-start.6 = (bf16[1024,4,64]{0,2,1:T(8,128)(2,1)S(1)}, bf16[1024,4,64]{0,2,1:T(8,128)(2,1)}, u32[]{:S(2)}) copy-start(bf16[1024,4,64]{0,2,1:T(8,128)(2,1)} %copy-done.5) | copy-start | bytes 1572868
  167.4 26.1 %copy-start.10 = (bf16[1024,4,64]{0,2,1:T(8,128)(2,1)S(1)}, bf16[1024,4,64]{0,2,1:T(8,128)(2,1)}, u32[]{:S(2)}) copy-start(bf16[1024,4,64]{0,2,1:T(8,128)(2,1)} %copy-done.9) | copy-start | bytes 1572868
  167.4 28.0 %copy-start.13 = (bf16[1024,4,64]{0,2,1:T(8,128)(2,1)S(1)}, bf16[1024,4,64]{0,2,1:T(8,128)(2,1)}, u32[]{:S(2)}) copy-start(bf16[1024,4,64]{0,2,1:T(8,128)(2,1)} %copy-done.12) | copy-start | bytes 1572868
  167.4 36.0 %collective-permute-start.16 = (bf16[1024,4,64]{0,2,1:T(8,128)(2,1)}, bf16[1024,4,64]{0,2,1:T(8,128)(2,1)S(1)}, u32[]{:S(2)}, u32[]{:S(2)}) collective-permute-start(bf16[1024,4,64]{0,2,1:T(8,128)(2,1)} %collective-permute-done.15), channel_id=1, source_target_pairs={{0,15},{1,0},{2,1},{3,2},{4,3},{5,4},{6,5},{7,6},{8,7},{9,8},{10,9... | collective-permute-start | bytes 1572872 | tf_op jit(solution)/shard_map/ppermute | solution.py:26
  175.2 22.1 %copy-start.16 = (bf16[1024,4,64]{0,2,1:T(8,128)(2,1)S(1)}, bf16[1024,4,64]{0,2,1:T(8,128)(2,1)}, u32[]{:S(2)}) copy-start(bf16[1024,4,64]{0,2,1:T(8,128)(2,1)} %copy-done.15) | copy-start | bytes 1572868
  225.5 6.1 copy-start.20
  242.6 11.7 %copy-start.3 = (bf16[64,4,1024]{2,0,1:T(8,128)(2,1)S(1)}, bf16[64,4,1024]{2,0,1:T(8,128)(2,1)}, u32[]{:S(2)}) copy-start(bf16[64,4,1024]{2,0,1:T(8,128)(2,1)} %convert_element_type.26) | copy-start | bytes 1572868
  385.7 2.0 copy-start.2
  705.7 8.1 %copy-start.19 = (f32[8,128,128]{1,2,0:T(8,128)}, f32[8,128,128]{1,2,0:T(8,128)S(1)}, u32[]{:S(2)}) copy-start(f32[8,128,128]{1,2,0:T(8,128)S(1)} %custom-call.70) | copy-start | bytes 1572868
  714.1 9.1 %copy-start.1 = (bf16[1,1024,1024]{2,1,0:T(8,128)(2,1)S(1)}, bf16[1,1024,1024]{2,1,0:T(8,128)(2,1)}, u32[]{:S(2)}) copy-start(bf16[1,1024,1024]{2,1,0:T(8,128)(2,1)} %param.13) | copy-start | bytes 6291460
Sparse Core Ops, SparseCore 0:
  10.5 112.2 all-gather.4
  125.2 109.1 all-gather.6
  260.5 115.3 all-reduce.2
